TPU v7x, 256 devices: a whole 4x4x8 slice. The times are simulated.
256 devices in a mesh: dp: 32 (over z, x), seq: 8 (over y, core).
Axes of the slice: x: 4, y: 4, z: 8, core: 2. Of those that a mesh axis runs over, the one named last changes fastest.
Arguments:
- query: bfloat16 [32768, 2048], P(('dp', 'seq')), may hold values from -6 to 6
- key_rows: bfloat16 [32768, 1024], P(('dp', 'seq')), may hold values from -6 to 6
- value_rows: bfloat16 [32768, 1024], P(('dp', 'seq')), may hold values from -6 to 6
- attn_out: bfloat16 [32768, 2048], P(('dp', 'seq')), may hold values from -6 to 6
- out_grad: bfloat16 [32768, 2048], P(('dp', 'seq')), may hold values from -6 to 6
- source_row: int32 [32768], P(('dp', 'seq')), may hold values from 0 to 32767, as said below
- segment_ids: int32 [32768], P('dp'), may hold values from 0 to 7, as said below
Outputs:
- grad_query: bfloat16 [32768, 2048], P(('dp', 'seq'))
- grad_key: bfloat16 [32768, 1024], P(('dp', 'seq'))
- grad_value: bfloat16 [32768, 1024], P(('dp', 'seq'))
Inputs may be any that keep to these rules, and one draw needn't show every extreme that they name: source_row is a permutation of all rows; a row keeps its seq index; one rollout device sends at most 8 rows to one owner, and every owner takes exactly 8 rows from some rollout device; within one seq index, how many rows go from one device to another depends only on the difference of their dp indices. `segment_ids`: within each pack of 1024 rows the ids start at 0, never fall and rise by at most 1 from one row to the next; every pack holds exactly 8 pairs.
All inputs are finite; a program needn't handle non-finite values.
Results may differ from a plain program's by a relative error of at most 0.0049.
Values may be sent and summed in bfloat16 or wider, within the bound.
No kernel may reach another device: no remote copies, remote signals or barrier semaphores. Data moves between devices by JAX's collectives and lax.ppermute only.
A program may use at most 64 MiB of HBM per device.

v0:
```python
import jax
import jax.numpy as jnp
from jax import lax
from jax.sharding import PartitionSpec as P

HEAD_DIM = 128


scaling = 1.0 / 12.0
softcap = 50.0


def arrival_slots(lists, rows_dev, seq_count, dp_count, capacity):
    source_dp = lists // rows_dev // seq_count
    matches = (
        source_dp[:, :, None] == jnp.arange(dp_count, dtype=jnp.int32)[None, None, :]
    ).astype(jnp.int32)
    arrival_rank = jnp.sum(jnp.cumsum(matches, axis=1) * matches, axis=2) - 1
    offsets = jnp.arange(lists.shape[0], dtype=jnp.int32)[:, None] * (dp_count * capacity)
    return offsets + source_dp * capacity + arrival_rank


def tile_scores(query_blk, key_blk, allowed):
    score = jnp.dot(query_blk, key_blk.T, preferred_element_type=jnp.float32) * scaling
    squashed = jnp.tanh(score / softcap)
    weights = jnp.where(allowed, jnp.exp(softcap * squashed), jnp.float32(0.0))
    return (squashed, weights)


def tile_total(operands):
    query_blk, key_blk, allowed = operands
    return jnp.sum(tile_scores(query_blk, key_blk, allowed)[1], axis=1, keepdims=True)


def tile_total_none(operands):
    return jnp.zeros((operands[0].shape[0], 1), jnp.float32)


def tile_grads(operands):
    query_blk, key_blk, value_blk, grad_blk, row_delta, row_total, allowed = operands
    squashed, weights = tile_scores(query_blk, key_blk, allowed)
    probabilities = weights / row_total
    prob_low = probabilities.astype(jnp.bfloat16)
    value_part = jnp.dot(prob_low.T, grad_blk, preferred_element_type=jnp.float32)
    prob_grad = jnp.dot(grad_blk, value_blk.T, preferred_element_type=jnp.float32)
    score_grad = (probabilities * (prob_grad - row_delta) * (1.0 - squashed * squashed)).astype(
        jnp.bfloat16
    )
    query_part = jnp.dot(score_grad, key_blk, preferred_element_type=jnp.float32) * scaling
    key_part = jnp.dot(score_grad.T, query_blk, preferred_element_type=jnp.float32) * scaling
    return (query_part, key_part, value_part)


def tile_grads_none(operands):
    query_blk = operands[0]
    key_blk = operands[1]
    return (
        jnp.zeros((query_blk.shape[0], query_blk.shape[1]), jnp.float32),
        jnp.zeros((key_blk.shape[0], key_blk.shape[1]), jnp.float32),
        jnp.zeros((key_blk.shape[0], key_blk.shape[1]), jnp.float32),
    )


def attend_grads(head_block, segments, query_width, key_width):
    group_rows = head_block.shape[0]
    head_count = query_width // HEAD_DIM
    block_rows = min(512, group_rows)
    block_count = group_rows // block_rows
    queries = head_block[:, :query_width]
    keys = head_block[:, query_width : query_width + key_width]
    values = head_block[:, query_width + key_width : query_width + 2 * key_width]
    outputs = head_block[:, query_width + 2 * key_width : 2 * query_width + 2 * key_width]
    grads = head_block[:, 2 * query_width + 2 * key_width :]
    position = jnp.arange(group_rows, dtype=jnp.int32)
    key_totals = [jnp.zeros((group_rows, HEAD_DIM), jnp.float32)]
    value_totals = [jnp.zeros((group_rows, HEAD_DIM), jnp.float32)]
    query_heads = []
    for head_index in range(head_count):
        kv_index = head_index // 2
        cols = slice(head_index * HEAD_DIM, (head_index + 1) * HEAD_DIM)
        kv_cols = slice(kv_index * HEAD_DIM, (kv_index + 1) * HEAD_DIM)
        query_blocks = []
        for block_index in range(block_count):
            rows = slice(block_index * block_rows, (block_index + 1) * block_rows)
            query_blk = queries[rows, cols]
            grad_blk = grads[rows, cols]
            row_delta = jnp.sum(
                grad_blk.astype(jnp.float32) * outputs[rows, cols].astype(jnp.float32),
                axis=1,
                keepdims=True,
            )
            key_spans = [
                (key_block * block_rows, (key_block + 1) * block_rows)
                for key_block in range(block_index + 1)
            ]
            masks = []
            for first_key, last_key in key_spans:
                same_pair = segments[rows][:, None] == segments[first_key:last_key][None, :]
                causal = position[first_key:last_key][None, :] <= position[rows][:, None]
                masks.append(same_pair & causal)
            row_total = jnp.zeros((block_rows, 1), jnp.float32)
            for span_index in range(len(key_spans)):
                first_key, last_key = key_spans[span_index]
                operands = (query_blk, keys[first_key:last_key, kv_cols], masks[span_index])
                row_total = row_total + lax.cond(
                    jnp.any(masks[span_index]), tile_total, tile_total_none, operands
                )
            query_acc = jnp.zeros((block_rows, HEAD_DIM), jnp.float32)
            for span_index in range(len(key_spans)):
                first_key, last_key = key_spans[span_index]
                operands = (
                    query_blk,
                    keys[first_key:last_key, kv_cols],
                    values[first_key:last_key, kv_cols],
                    grad_blk,
                    row_delta,
                    row_total,
                    masks[span_index],
                )
                query_part, key_part, value_part = lax.cond(
                    jnp.any(masks[span_index]), tile_grads, tile_grads_none, operands
                )
                query_acc = query_acc + query_part
                key_totals[kv_index] = key_totals[kv_index].at[first_key:last_key].add(key_part)
                value_totals[kv_index] = (
                    value_totals[kv_index].at[first_key:last_key].add(value_part)
                )
            query_blocks.append(query_acc.astype(jnp.bfloat16))
        query_heads.append(jnp.concatenate(query_blocks, axis=0))
    grad_q = jnp.concatenate(query_heads, axis=1)
    grad_k = jnp.concatenate([total.astype(jnp.bfloat16) for total in key_totals], axis=1)
    grad_v = jnp.concatenate([total.astype(jnp.bfloat16) for total in value_totals], axis=1)
    return (grad_q, grad_k, grad_v)


def local(query, key_rows, value_rows, attn_out, out_grad, source_row, segment_ids):
    rows_dev = query.shape[0]
    dp_count = lax.axis_size("dp")
    seq_count = lax.axis_size("seq")
    query_width = query.shape[1] // seq_count
    key_width = key_rows.shape[1] // seq_count
    packed = jnp.concatenate(
        [
            query.reshape(rows_dev, seq_count, query_width),
            key_rows.reshape(rows_dev, seq_count, key_width),
            value_rows.reshape(rows_dev, seq_count, key_width),
            attn_out.reshape(rows_dev, seq_count, query_width),
            out_grad.reshape(rows_dev, seq_count, query_width),
        ],
        axis=2,
    )
    capacity = 2 * rows_dev // dp_count
    my_dp = lax.axis_index("dp")
    column_lists = lax.all_gather(source_row, "dp", axis=0, tiled=True)
    from_here = (column_lists // rows_dev // seq_count == my_dp).reshape(dp_count, rows_dev)
    send_rank = jnp.cumsum(from_here.astype(jnp.int32), axis=1) - 1
    send_slot = jnp.arange(dp_count, dtype=jnp.int32)[:, None] * capacity + send_rank
    local_row = jnp.where(
        from_here, (column_lists % rows_dev).reshape(dp_count, rows_dev), rows_dev
    )
    slot_of_row = (
        jnp.zeros((rows_dev,), jnp.int32)
        .at[local_row.reshape(-1)]
        .set(send_slot.reshape(-1), mode="drop")
    )
    outgoing = (
        jnp.zeros((dp_count * capacity,) + packed.shape[1:], packed.dtype)
        .at[slot_of_row]
        .set(packed)
    )
    arrived = lax.all_to_all(outgoing, "dp", split_axis=0, concat_axis=0, tiled=True)
    position = arrival_slots(
        source_row.reshape(1, rows_dev), rows_dev, seq_count, dp_count, capacity
    )
    owner_rows = arrived[position.reshape(-1)]
    head_rows = lax.all_to_all(owner_rows, "seq", split_axis=1, concat_axis=0, tiled=True)
    head_block = head_rows.reshape(head_rows.shape[0], head_rows.shape[2])
    grad_q, grad_k, grad_v = attend_grads(head_block, segment_ids, query_width, key_width)
    joined = jnp.concatenate([grad_q, grad_k, grad_v], axis=1)[:, None, :]
    returned = lax.all_to_all(joined, "seq", split_axis=0, concat_axis=1, tiled=True)
    grad_query = returned[:, :, :query_width].reshape(rows_dev, seq_count * query_width)
    grad_key = returned[:, :, query_width : query_width + key_width].reshape(
        rows_dev, seq_count * key_width
    )
    grad_value = returned[:, :, query_width + key_width :].reshape(rows_dev, seq_count * key_width)
    return (grad_query, grad_key, grad_value)


def solution(mesh):
    in_specs = (
        P(("dp", "seq"), None),
        P(("dp", "seq"), None),
        P(("dp", "seq"), None),
        P(("dp", "seq"), None),
        P(("dp", "seq"), None),
        P(("dp", "seq")),
        P("dp"),
    )
    out_specs = (P(("dp", "seq"), None), P(("dp", "seq"), None), P(("dp", "seq"), None))
    return jax.shard_map(local, mesh=mesh, in_specs=in_specs, out_specs=out_specs, check_vma=False)
```

profile of v0, /device:TPU:1, one launch (start us, length us, event | category | flops | bytes accessed | tf_op | source)
XLA Modules:
  0.0 270.2 jit_solution(14420589670298492128)
XLA Ops:
  0.7 33.8 %all-gather = s32[32,1,128]{2,1,0:T(1,128)S(1)} all-gather(s32[1,1,128]{2,1,0:T(1,128)} %bitcast.160), channel_id=1, replica_groups=mesh['dp'=32,'seq'=8] {'dp'}, dimensions={0}, use_global_device_ids=true | all-gather | bytes 16896 | tf_op jit(solution)/shard_map/all_gather | solution.py:154
  34.9 15.5 %scatter_custom_fusion = s32[128]{0:T(128)S(1)} fusion(s32[4096]{0:T(1024)S(1)} %compare_select_fusion, s32[4096]{0:T(1024)S(1)} %add_bitcast_fusion, s32[]{:T(128)} %constant.484.clone.1), kind=kCustom, calls=%fused_computation.186 | custom fusion | bytes 516 | tf_op jit(solution)/shard_map/scatter | solution.py:164
  50.4 1.2 copy.71
  52.4 2.5 broadcast_in_dim.108
  54.9 15.7 %scatter_fusion = bf16[256,8,1024]{2,1,0:T(8,128)(2,1)} fusion(bf16[256,8,1024]{2,1,0:T(8,128)(2,1)} %broadcast_in_dim.108, s32[128]{0:T(128)S(1)} %compare_select_fusion.2, bf16[128,8,1024]{2,1,0:T(8,128)(2,1)S(1)} %constant_dynamic-update-slice_fusion), kind=kCustom, calls=%fused_computation.2 | custom fusion | bytes 6291968 | tf_op jit(solution)/shard_map/scatter | solution.py:169
  70.6 5.7 %all-to-all-start = ((bf16[256,8,1024]{2,1,0:T(8,128)(2,1)}), bf16[256,8,1024]{2,1,0:T(8,128)(2,1)}, u32[]{:S(2)}, u32[]{:S(2)}) async-start(bf16[256,8,1024]{2,1,0:T(8,128)(2,1)} %scatter_fusion), calls=%async_computation | async-start | bytes 8388608 | tf_op jit(solution)/shard_map/all_to_all | solution.py:171
  76.9 84.1 %all-to-all-done = bf16[256,8,1024]{2,1,0:T(8,128)(2,1)} async-done(((bf16[256,8,1024]{2,1,0:T(8,128)(2,1)}), bf16[256,8,1024]{2,1,0:T(8,128)(2,1)}, u32[]{:S(2)}, u32[]{:S(2)}) %all-to-all-start) | async-done | bytes 4194336 | tf_op jit(solution)/shard_map/all_to_all | solution.py:171
  161.0 2.9 %gather_fusion = bf16[128,8,1024]{2,1,0:T(8,128)(2,1)S(1)} fusion(bf16[256,8,1024]{2,1,0:T(8,128)(2,1)} %all-to-all-done, s32[1024]{0:T(1024)S(1)} %pad_clamp_fusion), kind=kCustom, calls=%fused_computation | custom fusion | bytes 4194816 | tf_op jit(solution)/shard_map/gather | solution.py:175
  163.9 2.5 copy.56
  166.4 17.2 %all-to-all-start.1 = ((bf16[128,8,1024]{2,0,1:T(8,128)(2,1)}), bf16[128,8,1024]{2,0,1:T(8,128)(2,1)S(1)}, u32[]{:S(2)}, u32[]{:S(2)}) async-start(bf16[128,8,1024]{2,0,1:T(8,128)(2,1)} %copy.56), calls=%async_computation.1 | async-start | bytes 4194304 | tf_op jit(solution)/shard_map/all_to_all | solution.py:176
  183.6 1.6 compare_and_fusion
  187.2 22.8 %all-to-all-done.1 = bf16[128,8,1024]{2,0,1:T(8,128)(2,1)S(1)} async-done(((bf16[128,8,1024]{2,0,1:T(8,128)(2,1)}), bf16[128,8,1024]{2,0,1:T(8,128)(2,1)S(1)}, u32[]{:S(2)}, u32[]{:S(2)}) %all-to-all-start.1) | async-done | bytes 2097184 | tf_op jit(solution)/shard_map/all_to_all | solution.py:176
  209.9 1.4 fusion.104
  211.5 0.9 conditional.20
  211.9 0.5 fusion.61
  212.4 0.9 conditional.21
  212.8 0.5 fusion.66
  213.3 0.9 conditional.14
  213.3 0.3 copy.58
  213.7 0.5 fusion.18
  214.2 0.9 conditional.15
  214.2 0.3 copy.59
  214.6 0.5 fusion.23
  215.1 0.9 conditional.12
  215.1 0.3 copy.57
  215.5 0.5 fusion.4
  216.0 2.4 conditional.13
  216.7 0.6 fusion.8
  217.9 0.5 fusion.11
  218.4 0.6 copy-done.12
  219.1 3.0 %conditional.17 = (f32[512,128]{1,0:T(8,128)S(1)}, f32[512,128]{1,0:T(8,128)S(1)}, f32[512,128]{1,0:T(8,128)S(1)}) conditional(s32[]{:T(128)} %convert_element_type.129, () %tuple.165, (bf16[512,128]{1,0:T(8,128)(2,1)S(1)}, bf16[512,128]{1,0:T(8,128)(2,1)S(1)}, pred[512,512]{1,0:T(32,128)(4,1)S(1)}, f32[512,1]{0,1:T(1,128)S(1)}, ...), branch_computations={%region_23.24_spmd, %region_24.25_spmd} | conditional | flops 339345408 | bytes 7477300 | solution.py:120
  219.4 1.5 fusion.36
  221.6 0.5 fusion.38
  222.1 0.7 copy-done.5
  222.8 3.0 %conditional.16 = (f32[512,128]{1,0:T(8,128)S(1)}, f32[512,128]{1,0:T(8,128)S(1)}, f32[512,128]{1,0:T(8,128)S(1)}) conditional(s32[]{:T(128)} %convert_element_type.128, () %tuple.159, (bf16[512,128]{1,0:T(8,128)(2,1)S(1)}, bf16[512,128]{1,0:T(8,128)(2,1)S(1)}, pred[512,512]{1,0:T(32,128)(4,1)S(1)}, f32[512,1]{0,1:T(1,128)S(1)}, ...), branch_computations={%region_21.22_spmd, %region_22.23_spmd} | conditional | flops 339345408 | bytes 7477300 | solution.py:120
  223.2 1.5 fusion.27
  225.4 0.5 fusion.29
  226.1 0.8 copy-done.22
  226.9 2.0 conditional.23
  227.2 0.5 fusion.79
  228.4 0.5 fusion.81
  228.9 0.7 copy-done.10
  229.7 5.5 %conditional.22 = (f32[512,128]{1,0:T(8,128)}, f32[512,128]{1,0:T(8,128)}, f32[512,128]{1,0:T(8,128)}) conditional(s32[]{:T(128)} %convert_element_type.128, () %tuple.171, (bf16[512,128]{1,0:T(8,128)(2,1)S(1)}, bf16[512,128]{1,0:T(8,128)(2,1)S(1)}, pred[512,512]{1,0:T(32,128)(4,1)S(1)}, f32[512,1]{0,1:T(1,128)S(1)}, ...), branch_computations={%region_38.39_spmd, %region_39.40_spmd} | conditional | flops 339345408 | bytes 8001616 | solution.py:120
  230.4 1.5 fusion.70
  231.9 1.1 convolution_multiply_fusion.19
  233.0 1.0 convolution_multiply_fusion.20
  234.0 1.2 fusion.72
  235.2 0.8 conditional.18
  235.6 0.5 fusion.46
  236.2 3.2 %conditional.19 = (f32[512,128]{1,0:T(8,128)S(1)}, f32[512,128]{1,0:T(8,128)S(1)}, bf16[512,128]{1,0:T(8,128)(2,1)S(1)}) conditional(s32[]{:T(128)} %convert_element_type.122, () %tuple.167, (bf16[512,128]{1,0:T(8,128)(2,1)S(1)}, bf16[512,128]{1,0:T(8,128)(2,1)S(1)}, pred[512,512]{1,0:T(32,128)(4,1)S(1)}, f32[512,1]{0,1:T(1,128)S(1)}, ...), branch_computations={%region_28.29_spmd, %region_29.31_spmd} | conditional | flops 339541504 | bytes 7872564 | solution.py:120
  236.8 1.5 fusion.50
  239.0 0.5 fusion.53
  239.6 1.0 add_dynamic-update-slice_fusion.2
  240.6 1.0 fusion.87
  241.9 1.0 add_dynamic-update-slice_fusion
  243.0 1.0 add_convert_fusion
  244.2 0.5 broadcast.501
  244.7 1.5 reduce.25
  246.2 0.8 reshape.494
  247.0 18.3 %all_to_all.38 = bf16[8,2,32768]{2,1,0:T(2,128)(2,1)S(1)} all-to-all(bf16[8,2,32768]{2,1,0:T(2,128)(2,1)S(1)} %reshape.494), channel_id=1, replica_groups=mesh['dp'=32,'seq'=8] {'seq'}, dimensions={0} | all-to-all | bytes 2097152 | tf_op jit(solution)/shard_map/all_to_all | solution.py:180
  265.3 1.0 reshape.495
  267.1 1.0 copy.67
  268.3 0.9 copy.68
  269.3 0.9 copy.69
  (127 shorter events, 10.6 us)
Async XLA Ops:
  0.6 51.1 %copy-start.18 = (bf16[128,1024]{1,0:T(8,128)(2,1)S(1)}, bf16[128,1024]{1,0:T(8,128)(2,1)}, u32[]{:S(2)}) copy-start(bf16[128,1024]{1,0:T(8,128)(2,1)} %param.56) | copy-start | bytes 786436
  0.6 51.1 %copy-start.19 = (bf16[128,1024]{1,0:T(8,128)(2,1)S(1)}, bf16[128,1024]{1,0:T(8,128)(2,1)}, u32[]{:S(2)}) copy-start(bf16[128,1024]{1,0:T(8,128)(2,1)} %param.57) | copy-start | bytes 786436
  0.7 51.2 %copy-start.16 = (bf16[128,2048]{1,0:T(8,128)(2,1)S(1)}, bf16[128,2048]{1,0:T(8,128)(2,1)}, u32[]{:S(2)}) copy-start(bf16[128,2048]{1,0:T(8,128)(2,1)} %param.58) | copy-start | bytes 1572868
  50.4 1.6 copy-start.17
  70.6 5.7 %copy-start.30 = (s32[128]{0:T(128)S(1)}, s32[128]{0:T(128)}, u32[]{:S(2)}) copy-start(s32[128]{0:T(128)} %param.60) | copy-start | bytes 1540
  70.6 90.3 %all-to-all-start = ((bf16[256,8,1024]{2,1,0:T(8,128)(2,1)}), bf16[256,8,1024]{2,1,0:T(8,128)(2,1)}, u32[]{:S(2)}, u32[]{:S(2)}) async-start(bf16[256,8,1024]{2,1,0:T(8,128)(2,1)} %scatter_fusion), calls=%async_computation | async-start | bytes 8388608 | tf_op jit(solution)/shard_map/all_to_all | solution.py:171
  166.4 17.3 %copy-start.29 = (s32[1024]{0:T(1024)S(1)}, s32[1024]{0:T(1024)}, u32[]{:S(2)}) copy-start(s32[1024]{0:T(1024)} %param.61) | copy-start | bytes 12292
  166.4 43.6 %all-to-all-start.1 = ((bf16[128,8,1024]{2,0,1:T(8,128)(2,1)}), bf16[128,8,1024]{2,0,1:T(8,128)(2,1)S(1)}, u32[]{:S(2)}, u32[]{:S(2)}) async-start(bf16[128,8,1024]{2,0,1:T(8,128)(2,1)} %copy.56), calls=%async_computation.1 | async-start | bytes 4194304 | tf_op jit(solution)/shard_map/all_to_all | solution.py:176
  213.3 1.8 copy-start
  214.2 1.8 copy-start.3
  214.2 1.8 copy-start.4
  214.2 1.8 copy-start.21
  214.2 1.8 copy-start.28
  218.4 0.6 copy-start.12
  219.4 2.2 copy-start.26
  222.1 0.7 copy-start.5
  223.2 2.2 copy-start.27
  225.9 1.1 copy-start.7
  225.9 1.0 copy-start.22
  225.9 1.1 copy-start.25
  228.9 0.7 copy-start.10
  228.9 0.8 copy-start.9
  229.7 0.6 copy-start.23
  230.4 3.6 %copy-start.24 = (bf16[512,128]{1,0:T(8,128)(2,1)S(1)}, bf16[512,128]{1,0:T(8,128)(2,1)}, u32[]{:S(2)}) copy-start(bf16[512,128]{1,0:T(8,128)(2,1)} %copy-done.23) | copy-start | bytes 393220 | tf_op jit(solution)/shard_map/cond
  235.2 0.9 copy-start.1
  235.2 1.0 copy-start.2
  236.8 2.2 copy-start.20
  239.5 2.3 copy-start.14
  239.5 2.2 copy-start.6
  241.6 1.3 copy-start.11
  241.8 1.3 copy-start.8
  241.9 2.2 copy-start.13
  241.9 2.2 copy-start.15
where the time goes:
time: 271 us; the launch traced here: 270 us
  waiting for transfers between devices  107 us (39%)
  local copies, waits for them, and re-layouts  52.9 us (20%)
  blocking collectives  52.2 us (19%)
  starting transfers between devices  23 us (8%)
  matrix products  20.9 us (8%)
  other arithmetic  10.4 us (4%)
  between operations  3.32 us (1%)
    all_to_all x1, waiting for transfers between devices, local(): lax.all_to_all(outgoing, 'dp', split_axis=0, concat_axis=0, tiled=True)  84.1 us
    all_gather x1, blocking collectives, local(): column_lists = lax.all_gather(source_row, 'dp', axis=0, tiled=True)  33.8 us
    all_to_all x1, waiting for transfers between devices, local(): lax.all_to_all(owner_rows, 'seq', split_axis=1, concat_axis=0, tiled=True)  22.8 us
    all_to_all x1, blocking collectives, local(): lax.all_to_all(joined, 'seq', split_axis=0, concat_axis=1, tiled=True)  18.3 us
    all_to_all x1, starting transfers between devices, local(): lax.all_to_all(owner_rows, 'seq', split_axis=1, concat_axis=0, tiled=True)  17.2 us
    scatter x1, local copies, waits for them, and re-layouts, local(): outgoing = jnp.zeros((dp_count * capacity,) + packed.shape[1:], packed.dt...  15.7 us
    scatter x1, local copies, waits for them, and re-layouts, local(): slot_of_row = jnp.zeros((rows_dev,), jnp.int32).at[local_row.reshape(-1)]...  15.5 us
    unnamed x69, local copies, waits for them, and re-layouts  10 us
  transfers between devices with their start and end apart: 2, of which 2 were waited for; matrix products, arithmetic and copies ran while one was open for 1% of the time, Pallas kernels for 0%

commit v1 on v0

v1 whole, which is shorter than its diff:
```python
import functools

import jax
import jax.numpy as jnp
from jax import lax
from jax.experimental import pallas as pl
from jax.experimental.pallas import tpu as pltpu
from jax.sharding import PartitionSpec as P

HEAD_DIM = 128
N_DP = 32
N_SEQ = 8
N_Y = 4
ROWS = 128
GROUP = N_SEQ * ROWS
HALF = 3 * HEAD_DIM
LANES = 128
BLOCK = 256
CAPACITY = 56
EXTRA = 16
STEPS = 10
NEAR = 7

scaling = 1.0 / 12.0
softcap = 50.0

PARAMS = pltpu.CompilerParams(vmem_limit_bytes=28 * 1024 * 1024)
FULL = pltpu.CompilerParams(vmem_limit_bytes=60 * 1024 * 1024)
VMEM = pl.BlockSpec(memory_space=pltpu.VMEM)
SMEM = pl.BlockSpec(memory_space=pltpu.SMEM)
HBM = pl.BlockSpec(memory_space=pltpu.HBM)


def iota(shape, dim):
    return lax.broadcasted_iota(jnp.int32, shape, dim)


def float_iota(shape, dim):
    return iota(shape, dim).astype(jnp.float32)


def one_hot(hits):
    return hits.astype(jnp.float32).astype(jnp.bfloat16)


def nt_dot(left, right):
    return lax.dot_general(left, right, (((1,), (1,)), ((), ())), preferred_element_type=jnp.float32)


def nn_dot(left, right):
    return jnp.dot(left, right, preferred_element_type=jnp.float32)


def turned(rows):
    blank = jnp.zeros((LANES - rows.shape[0], LANES), jnp.float32)
    return jnp.concatenate([rows, blank], axis=0).T


def wide(rows):
    return jnp.concatenate([rows[s : s + 1] for s in range(N_SEQ)], axis=1)


def request_kernel(list_ref, request_ref):
    listed = list_ref[...]
    source = (listed // GROUP).astype(jnp.float32)
    local_row = (listed % ROWS).astype(jnp.float32)
    before = iota((ROWS, ROWS), 0) < iota((ROWS, ROWS), 1)
    hits = ((turned(source)[:, 0:1] == source) & before).astype(jnp.float32)
    rank = jnp.sum(hits, axis=0, keepdims=True)
    pick = one_hot(turned(rank)[:, 0:1] == float_iota((ROWS, LANES), 1))
    from_source = float_iota((N_DP, ROWS), 0) == source
    table = nn_dot(jnp.where(from_source, local_row + 1.0, 0.0).astype(jnp.bfloat16), pick)
    request_ref[...] = table.astype(jnp.int32)


def pack_near_kernel(list_ref, request_ref, query_hbm, key_hbm, packed_ref, query_ref, key_ref, sems):
    copies = [
        pltpu.make_async_copy(query_hbm, query_ref, sems.at[0]),
        pltpu.make_async_copy(key_hbm, key_ref, sems.at[1]),
    ]
    for copy in copies:
        copy.start()
    listed = list_ref[...]
    source = (listed // GROUP).astype(jnp.float32)
    local_row = (listed % ROWS).astype(jnp.float32)
    wanted = request_ref[...].astype(jnp.float32) - 1.0
    row_id = float_iota((N_DP, ROWS), 1)
    owner_id = float_iota((N_DP, ROWS), 0)
    owner = jnp.zeros((1, ROWS), jnp.float32)
    rank = jnp.zeros((1, ROWS), jnp.float32)
    for k in range(8):
        hits = (wanted[:, k : k + 1] == row_id).astype(jnp.float32)
        owner = owner + jnp.sum(hits * owner_id, axis=0, keepdims=True)
        rank = rank + float(k) * jnp.sum(hits, axis=0, keepdims=True)
    tail = jnp.concatenate([owner, rank, source, local_row, jnp.zeros((4, LANES), jnp.float32)], axis=0)
    tail = jnp.concatenate([tail, jnp.zeros((8, HALF - LANES), jnp.float32)], axis=1)
    for copy in copies:
        copy.wait()
    for group in range(N_SEQ):
        two = slice(2 * group * HEAD_DIM, 2 * (group + 1) * HEAD_DIM)
        one = slice(group * HEAD_DIM, (group + 1) * HEAD_DIM)
        rows = jnp.concatenate([query_ref[:, two], key_ref[:, one]], axis=1)
        packed_ref[group] = jnp.concatenate([rows.astype(jnp.float32), tail], axis=0).astype(
            jnp.bfloat16
        )


def pack_far_kernel(ids_ref, value_hbm, out_hbm, grad_hbm, *refs):
    packed_refs, (value_ref, out_ref, grad_ref, delta_ref, sems) = refs[:N_Y], refs[N_Y:]
    copies = [
        pltpu.make_async_copy(grad_hbm, grad_ref, sems.at[0]),
        pltpu.make_async_copy(out_hbm, out_ref, sems.at[1]),
        pltpu.make_async_copy(value_hbm, value_ref, sems.at[2]),
    ]
    for copy in copies:
        copy.start()
    copies[0].wait()
    copies[1].wait()
    lane = iota((ROWS, LANES), 1)
    table = jnp.zeros((ROWS, LANES), jnp.float32)
    for head in range(2 * N_SEQ):
        cols = slice(head * HEAD_DIM, (head + 1) * HEAD_DIM)
        product = grad_ref[:, cols].astype(jnp.float32) * out_ref[:, cols].astype(jnp.float32)
        table = jnp.where(lane == head, jnp.sum(product, axis=1, keepdims=True), table)
    delta = table.T
    high = delta.astype(jnp.bfloat16).astype(jnp.float32)
    low = delta - high
    for group in range(N_SEQ):
        pair = slice(2 * group, 2 * group + 2)
        delta_ref[group] = jnp.concatenate(
            [high[pair], low[pair], jnp.zeros((4, LANES), jnp.float32)], axis=0
        )
    copies[2].wait()
    for m in range(N_SEQ):
        group = jnp.bitwise_xor(ids_ref[0], m)
        two = pl.ds(pl.multiple_of(group * 256, 256), 256)
        one = pl.ds(pl.multiple_of(group * 128, 128), 128)
        rows = jnp.concatenate([value_ref[:, one], grad_ref[:, two]], axis=1)
        tail = jnp.concatenate(
            [delta_ref[group], jnp.zeros((8, HALF - LANES), jnp.float32)], axis=1
        )
        packed_refs[m // 2][m % 2] = jnp.concatenate(
            [rows.astype(jnp.float32), tail], axis=0
        ).astype(jnp.bfloat16)


def place_rows(tails, place_ref):
    counts = jnp.zeros((N_DP, 1), jnp.float32)
    for s in range(N_SEQ):
        owner = tails[s][0:1]
        to_owner = (float_iota((N_DP, ROWS), 0) == owner).astype(jnp.float32)
        base = jnp.sum(to_owner * counts, axis=0, keepdims=True)
        counts = counts + jnp.sum(to_owner, axis=1, keepdims=True)
        slot = tails[s][1:2] + base + 1.0
        place_ref[:, s * ROWS : (s + 1) * ROWS] = jnp.concatenate(
            [owner, slot, jnp.zeros((6, LANES), jnp.float32)], axis=0
        )
    return counts


def group_picks(place_ref, group, first, capacity):
    owner = place_ref[0:1, :]
    slot = place_ref[1:2, :] - float(first)
    place = owner * float(capacity) + slot
    place = jnp.where((slot >= 0.0) & (slot < capacity), place, -1.0)
    place = place - float(8 * capacity * group)
    return one_hot(float_iota((8 * capacity, GROUP), 0) == place)


def send_near_kernel(rows_ref, sent_ref, place_ref, most_ref, ext_ref):
    group_rows = 8 * CAPACITY
    tails = []
    for s in range(N_SEQ):
        whole = rows_ref[s]
        ext_ref[s * ROWS : (s + 1) * ROWS, :] = whole[:ROWS]
        tails.append(whole[ROWS:, :LANES].astype(jnp.float32))
    counts = place_rows(tails, place_ref)
    most_ref[0, 0] = jnp.max(counts).astype(jnp.int32)
    for group in range(N_DP // 8):
        pick = group_picks(place_ref, group, 0, CAPACITY)
        rows = slice(group * group_rows, (group + 1) * group_rows)
        sent_ref[rows, :] = nn_dot(pick, ext_ref[...]).astype(jnp.bfloat16)


def join_far(ids_ref, straight, crossed_ref, ext_ref, delta_ref):
    for m in range(N_SEQ):
        column = jnp.bitwise_xor(ids_ref[0], m)
        whole = crossed_ref[m // 2] if m % 2 else straight[m // 2][0]
        ext_ref[pl.ds(pl.multiple_of(column * ROWS, ROWS), ROWS), :] = whole[:ROWS]
        if delta_ref is not None:
            delta_ref[column] = whole[ROWS:, :LANES].astype(jnp.float32)


def send_far_kernel(ids_ref, place_ref, *refs):
    straight, (crossed_ref, sent_ref, ext_ref, delta_ref) = refs[:N_Y], refs[N_Y:]
    group_rows = 8 * CAPACITY
    join_far(ids_ref, straight, crossed_ref, ext_ref, delta_ref)
    delta = jnp.concatenate([delta_ref[s] for s in range(N_SEQ)], axis=1)
    owner = place_ref[0:1, :]
    slot_cols = [
        turned(place_ref[:, s * ROWS : (s + 1) * ROWS])[:, 1:2] for s in range(N_SEQ)
    ]
    slot_col = jnp.concatenate(slot_cols, axis=0)
    lane = float_iota((GROUP, LANES), 1)
    to_owner = float_iota((N_DP, GROUP), 0) == owner
    tail = jnp.zeros((2 * N_DP, LANES), jnp.float32)
    for head in range(2):
        spread = jnp.concatenate(
            [jnp.where(to_owner, delta[c : c + 1], 0.0) for c in (head, 2 + head)], axis=0
        )
        slot_pick = one_hot(slot_col + (64.0 * head - 1.0) == lane)
        tail = tail + nn_dot(spread.astype(jnp.bfloat16), slot_pick)
    tail = jnp.concatenate([tail[:N_DP], tail[N_DP:]], axis=1)
    for group in range(N_DP // 8):
        pick = group_picks(place_ref, group, 0, CAPACITY)
        rows = slice(group * group_rows, (group + 1) * group_rows)
        sent_ref[rows, :] = nn_dot(pick, ext_ref[...]).astype(jnp.bfloat16)
    row = iota((16, 2 * LANES), 0)
    for dp in range(N_DP):
        inside = dp * CAPACITY % 16
        rows = slice(dp * CAPACITY - inside, dp * CAPACITY - inside + 16)
        kept = sent_ref[rows, : 2 * LANES].astype(jnp.float32)
        mine = jnp.broadcast_to(tail[dp : dp + 1], (16, 2 * LANES))
        sent_ref[rows, : 2 * LANES] = jnp.where(row == inside, mine, kept).astype(jnp.bfloat16)


def send_extra_kernel(ids_ref, place_ref, rows_ref, *refs):
    straight, (crossed_ref, sent_ref, near_ref, far_ref) = refs[:N_Y], refs[N_Y:]
    group_rows = 8 * EXTRA
    for s in range(N_SEQ):
        whole = rows_ref[s]
        near_ref[s * ROWS : (s + 1) * ROWS, :] = whole[:ROWS]
    join_far(ids_ref, straight, crossed_ref, far_ref, None)
    for group in range(N_DP // 8):
        pick = group_picks(place_ref, group, CAPACITY, EXTRA)
        rows = slice(group * group_rows, (group + 1) * group_rows)
        sent_ref[rows, :HALF] = nn_dot(pick, near_ref[...]).astype(jnp.bfloat16)
        sent_ref[rows, HALF:] = nn_dot(pick, far_ref[...]).astype(jnp.bfloat16)


def index_kernel(segment_ref, head_ref, rows_ref, cols_ref):
    sources = []
    for s in range(N_SEQ):
        whole = head_ref[s]
        sources.append(whole[ROWS:, :LANES].astype(jnp.float32)[2:3])
    source = jnp.concatenate(sources, axis=0)
    segment = segment_ref[...].astype(jnp.float32)
    source_cols = turned(source)
    before = iota((ROWS, ROWS), 0) < iota((ROWS, ROWS), 1)
    slots = []
    for s in range(N_SEQ):
        mine = source[s : s + 1]
        hits = ((source_cols[:, s : s + 1] == mine) & before).astype(jnp.float32)
        for earlier in range(s):
            hits = hits + (source_cols[:, earlier : earlier + 1] == mine).astype(jnp.float32)
        slots.append(jnp.sum(hits, axis=0, keepdims=True))
    slot = jnp.concatenate(slots, axis=0)
    columns = turned(jnp.concatenate([source, slot, segment], axis=0))
    lane = iota((ROWS, LANES), 1)
    for s in range(N_SEQ):
        column = jnp.where(lane == 0, columns[:, s : s + 1], 0.0)
        column = jnp.where(lane == 1, columns[:, 8 + s : 9 + s], column)
        column = jnp.where(lane == 2, columns[:, 16 + s : 17 + s], column)
        cols_ref[s * ROWS : (s + 1) * ROWS, :] = column
    rows_ref[0:8, :] = source
    rows_ref[8:16, :] = slot
    rows_ref[16:24, :] = segment


def to_owner_order(cols_ref, arrived_ref, x_ref):
    slots = N_DP * CAPACITY
    slot_id = float_iota((BLOCK, slots), 1)
    for block in range(GROUP // BLOCK):
        rows = slice(block * BLOCK, (block + 1) * BLOCK)
        slot = cols_ref[rows, 1:2] + 1.0
        place = jnp.where(slot < CAPACITY, cols_ref[rows, 0:1] * float(CAPACITY) + slot, -1.0)
        x_ref[rows, :] = nn_dot(one_hot(place == slot_id), arrived_ref[...]).astype(jnp.bfloat16)


def add_extra(most_ref, cols_ref, extra_hbm, extra_ref, sem, x_ref, span):
    @pl.when(most_ref[0, 0] >= CAPACITY)
    def _():
        copy = pltpu.make_async_copy(extra_hbm, extra_ref, sem)
        copy.start()
        copy.wait()
        slot_id = float_iota((BLOCK, N_DP * EXTRA), 1)
        for block in range(GROUP // BLOCK):
            rows = slice(block * BLOCK, (block + 1) * BLOCK)
            slot = cols_ref[rows, 1:2] - float(CAPACITY - 1)
            place = jnp.where(slot >= 0.0, cols_ref[rows, 0:1] * float(EXTRA) + slot, -1.0)
            found = nn_dot(one_hot(place == slot_id), extra_ref[:, span])
            x_ref[rows, :] += found.astype(jnp.bfloat16)


def near_rows(block):
    if block == 0:
        return slice(0, BLOCK)
    return slice((2 * block - 1) * BLOCK, (2 * block + 1) * BLOCK)


def far_rows(block, key_block):
    step = NEAR + (0 if block == 2 else 1 + key_block)
    return slice(step * BLOCK, (step + 1) * BLOCK)


def reaches(segment_ref, block, key_block):
    return segment_ref[(key_block + 1) * BLOCK - 1] == segment_ref[block * BLOCK]


def weigh_kernel(
    segment_ref, most_ref, arrived_ref, extra_hbm, rows_ref, cols_ref,
    x_ref, kt_ref, low_ref, slope_ref, extra_ref, weight_ref, squash_ref, total_ref, sem,
):
    to_owner_order(cols_ref, arrived_ref, x_ref)
    add_extra(most_ref, cols_ref, extra_hbm, extra_ref, sem, x_ref, slice(0, HALF))
    segment = wide(rows_ref[16:24, :])
    for block in range(GROUP // BLOCK):
        rows = slice(block * BLOCK, (block + 1) * BLOCK)
        kt_ref[:, rows] = x_ref[rows, 256:384].astype(jnp.float32).T.astype(jnp.bfloat16)
    for block in range(GROUP // BLOCK):
        rows = slice(block * BLOCK, (block + 1) * BLOCK)
        near = slice(max(block - 1, 0) * BLOCK, (block + 1) * BLOCK)
        near_count = near.stop - near.start
        queries = jnp.concatenate([x_ref[rows, 0:128], x_ref[rows, 128:256]], axis=0)
        segment_q = jnp.concatenate([segment[:, rows]] * 2, axis=1)
        far = range(block - 1)

        def weigh(keys, causal):
            score = nt_dot(x_ref[keys, 256:384], queries)
            squashed = jnp.tanh(score * (scaling / softcap))
            allowed = cols_ref[keys, 2:3] == segment_q
            if causal is not None:
                allowed = allowed & causal
            return squashed, jnp.where(allowed, jnp.exp(softcap * squashed), 0.0)

        def finish(held, squashed, weights, inverse):
            probabilities = weights * inverse
            low_ref[held, :] = probabilities.astype(jnp.bfloat16)
            slope_ref[held, :] = probabilities * (1.0 - squashed * squashed)

        if len(far) > 0:
            total_ref[...] = jnp.zeros_like(total_ref)
        for key_block in far:

            @pl.when(reaches(segment_ref, block, key_block))
            def _(keys=slice(key_block * BLOCK, (key_block + 1) * BLOCK)):
                squashed, weights = weigh(keys, None)
                weight_ref[keys, :] = weights
                squash_ref[keys, :] = squashed
                total_ref[0:1, :] += jnp.sum(weights, axis=0, keepdims=True)

        ahead = iota((near_count, BLOCK), 0) - iota((near_count, BLOCK), 1)
        causal = (ahead <= near_count - BLOCK).astype(jnp.float32)
        causal = jnp.concatenate([causal, causal], axis=1) > 0.0
        squashed, weights = weigh(near, causal)
        total = jnp.sum(weights, axis=0, keepdims=True)
        if len(far) > 0:
            total = total + total_ref[0:1, :]
        inverse = 1.0 / total
        finish(near_rows(block), squashed, weights, inverse)
        if len(far) > 0:
            total_ref[0:1, :] = inverse
        for key_block in far:

            @pl.when(reaches(segment_ref, block, key_block))
            def _(
                keys=slice(key_block * BLOCK, (key_block + 1) * BLOCK),
                held=far_rows(block, key_block),
            ):
                finish(held, squash_ref[keys, :], weight_ref[keys, :], total_ref[0:1, :])


def back_kernel(
    segment_ref, most_ref, arrived_ref, extra_hbm, rows_ref, cols_ref,
    x_hbm, kt_hbm, low_hbm, slope_hbm, out_ref,
    extra_ref, x_ref, kt_ref, low_ref, slope_ref, y_ref, lanes_ref, gqt_ref, gk_ref, gv_ref, sems,
):
    fetched = slice(0, NEAR * BLOCK)
    copies = [
        pltpu.make_async_copy(low_hbm.at[fetched], low_ref.at[fetched], sems.at[0]),
        pltpu.make_async_copy(slope_hbm.at[fetched], slope_ref.at[fetched], sems.at[1]),
        pltpu.make_async_copy(x_hbm, x_ref, sems.at[2]),
        pltpu.make_async_copy(kt_hbm, kt_ref, sems.at[3]),
    ]
    for copy in copies:
        copy.start()
    to_owner_order(cols_ref, arrived_ref, y_ref)
    add_extra(most_ref, cols_ref, extra_hbm, extra_ref, sems.at[4], y_ref, slice(HALF, 2 * HALF))
    slots = N_DP * CAPACITY
    first = one_hot(iota((LANES, slots), 0) * CAPACITY == iota((LANES, slots), 1))
    parts = nn_dot(first, arrived_ref[:, : 2 * LANES])
    from_source = one_hot(float_iota((LANES, GROUP), 0) == wide(rows_ref[0:8, :]))
    slot = wide(rows_ref[8:16, :])
    high = parts[:, :LANES].T.astype(jnp.bfloat16)
    low = parts[:, LANES:].T.astype(jnp.bfloat16)
    both = nn_dot(high, from_source) + nn_dot(low, from_source)
    place = float_iota((LANES, GROUP), 0)
    for head in range(2):
        lanes_ref[head : head + 1, :] = jnp.sum(
            jnp.where(place == slot + 64.0 * head, both, 0.0), axis=0, keepdims=True
        )
    gk_ref[...] = jnp.zeros_like(gk_ref)
    gv_ref[...] = jnp.zeros_like(gv_ref)
    for copy in copies:
        copy.wait()
    for block in range(GROUP // BLOCK):
        rows = slice(block * BLOCK, (block + 1) * BLOCK)
        near = slice(max(block - 1, 0) * BLOCK, (block + 1) * BLOCK)
        queries = jnp.concatenate([x_ref[rows, 0:128], x_ref[rows, 128:256]], axis=0)
        grads = jnp.concatenate([y_ref[rows, 128:256], y_ref[rows, 256:384]], axis=0)
        delta = jnp.concatenate([lanes_ref[0:1, rows], lanes_ref[1:2, rows]], axis=1)

        def back(keys, held):
            gv_ref[keys, :] += nn_dot(low_ref[held, :], grads)
            prob_grad = nt_dot(y_ref[keys, 0:128], grads)
            score_grad = (slope_ref[held, :] * (prob_grad - delta)).astype(jnp.bfloat16)
            gk_ref[keys, :] += nn_dot(score_grad, queries)
            return nn_dot(kt_ref[:, keys], score_grad)

        gqt_ref[...] = back(near, near_rows(block))
        for key_block in range(block - 1):

            @pl.when(reaches(segment_ref, block, key_block))
            def _(
                keys=slice(key_block * BLOCK, (key_block + 1) * BLOCK),
                held=far_rows(block, key_block),
            ):
                late = [
                    pltpu.make_async_copy(low_hbm.at[held], low_ref.at[held], sems.at[0]),
                    pltpu.make_async_copy(slope_hbm.at[held], slope_ref.at[held], sems.at[1]),
                ]
                for copy in late:
                    copy.start()
                for copy in late:
                    copy.wait()
                gqt_ref[...] += back(keys, held)

        turned_back = (gqt_ref[...].T * scaling).astype(jnp.bfloat16)
        out_ref[rows, 0:128] = turned_back[:BLOCK]
        out_ref[rows, 128:256] = turned_back[BLOCK:]
    out_ref[:, 256:384] = (gk_ref[...] * scaling).astype(jnp.bfloat16)
    out_ref[:, 384:512] = gv_ref[...].astype(jnp.bfloat16)


def unpack_kernel(returned_ref, query_ref, key_ref, value_ref):
    for group in range(N_SEQ):
        two = slice(2 * group * HEAD_DIM, 2 * (group + 1) * HEAD_DIM)
        one = slice(group * HEAD_DIM, (group + 1) * HEAD_DIM)
        query_ref[:, two] = returned_ref[group, :, 0:256]
        key_ref[:, one] = returned_ref[group, :, 256:384]
        value_ref[:, one] = returned_ref[group, :, 384:512]


def shape(dims, dtype=jnp.bfloat16):
    return jax.ShapeDtypeStruct(dims, dtype)


def call(kernel, name, out_shape, in_specs, out_specs, scratch=(), params=PARAMS, flops=0):
    estimate = pl.CostEstimate(flops=flops, bytes_accessed=4_000_000, transcendentals=0)
    return pl.pallas_call(
        kernel,
        out_shape=out_shape,
        in_specs=in_specs,
        out_specs=out_specs,
        scratch_shapes=list(scratch),
        compiler_params=params,
        cost_estimate=estimate if flops else None,
        name=name,
    )


def rows_vmem(dims, dtype=jnp.bfloat16):
    return pltpu.VMEM(dims, dtype)


PACKED = (ROWS + 8, HALF)
HELD = (STEPS * BLOCK, 2 * BLOCK)
SLOTS = (N_DP * CAPACITY, HALF)

make_request = call(request_kernel, "request", shape((N_DP, LANES), jnp.int32), [VMEM], VMEM)
pack_near = call(
    pack_near_kernel, "pack_near", shape((N_SEQ,) + PACKED), [VMEM, VMEM, HBM, HBM], VMEM,
    [rows_vmem((ROWS, 2048)), rows_vmem((ROWS, 1024)), pltpu.SemaphoreType.DMA((2,))], FULL,
)
pack_far = call(
    pack_far_kernel, "pack_far", [shape((2,) + PACKED)] * N_Y, [SMEM, HBM, HBM, HBM], [VMEM] * N_Y,
    [
        rows_vmem((ROWS, 1024)), rows_vmem((ROWS, 2048)), rows_vmem((ROWS, 2048)),
        rows_vmem((N_SEQ, 8, LANES), jnp.float32), pltpu.SemaphoreType.DMA((3,)),
    ],
    FULL,
)
send_near = call(
    send_near_kernel, "send_near",
    [shape(SLOTS), shape((8, GROUP), jnp.float32), shape((1, 1), jnp.int32)],
    [VMEM], [VMEM, VMEM, SMEM], [rows_vmem((GROUP, HALF))], flops=1_400_000_000,
)
send_far = call(
    send_far_kernel, "send_far", shape(SLOTS), [SMEM] + [VMEM] * (2 + N_Y), VMEM,
    [rows_vmem((GROUP, HALF)), rows_vmem((N_SEQ, 8, LANES), jnp.float32)], flops=1_400_000_000,
)
send_extra = call(
    send_extra_kernel, "send_extra", shape((N_DP * EXTRA, 2 * HALF)), [SMEM] + [VMEM] * (3 + N_Y), VMEM,
    [rows_vmem((GROUP, HALF)), rows_vmem((GROUP, HALF))],
)
make_index = call(
    index_kernel, "index",
    [shape((24, LANES), jnp.float32), shape((GROUP, LANES), jnp.float32)], [VMEM, VMEM], [VMEM, VMEM],
    flops=200_000_000,
)
weigh = call(
    weigh_kernel, "weigh",
    [shape((GROUP, HALF)), shape((HEAD_DIM, GROUP)), shape(HELD), shape(HELD, jnp.float32)],
    [SMEM, SMEM, VMEM, HBM, VMEM, VMEM], [VMEM] * 4,
    [
        rows_vmem((N_DP * EXTRA, 2 * HALF)),
        rows_vmem((GROUP - 2 * BLOCK, 2 * BLOCK), jnp.float32),
        rows_vmem((GROUP - 2 * BLOCK, 2 * BLOCK), jnp.float32),
        rows_vmem((8, 2 * BLOCK), jnp.float32),
        pltpu.SemaphoreType.DMA,
    ],
    flops=3_000_000_000,
)
back = call(
    back_kernel, "back", shape((GROUP, 4 * HEAD_DIM)),
    [SMEM, SMEM, VMEM, HBM, VMEM, VMEM, HBM, HBM, HBM, HBM], VMEM,
    [
        rows_vmem((N_DP * EXTRA, 2 * HALF)),
        rows_vmem((GROUP, HALF)),
        rows_vmem((HEAD_DIM, GROUP)),
        rows_vmem(HELD),
        rows_vmem(HELD, jnp.float32),
        rows_vmem((GROUP, HALF)),
        rows_vmem((8, GROUP), jnp.float32),
        rows_vmem((HEAD_DIM, 2 * BLOCK), jnp.float32),
        rows_vmem((GROUP, HEAD_DIM), jnp.float32),
        rows_vmem((GROUP, HEAD_DIM), jnp.float32),
        pltpu.SemaphoreType.DMA((5,)),
    ],
    FULL,
)
unpack = call(
    unpack_kernel, "unpack", [shape((ROWS, 2048)), shape((ROWS, 1024)), shape((ROWS, 1024))],
    [VMEM], [VMEM] * 3,
)


def relay(array):
    return lax.all_to_all(array, "dp", split_axis=0, concat_axis=0, tiled=True)


def swap(array, m):
    return lax.ppermute(array, "seq", [(s, s ^ m) for s in range(N_SEQ)]) if m else array


def local(query, key_rows, value_rows, attn_out, out_grad, source_row, segment_ids):
    ids = lax.axis_index("seq").reshape(1)
    listed = source_row.reshape(1, ROWS)
    asked = relay(make_request(listed))
    far = pack_far(ids, value_rows, attn_out, out_grad)
    asked, far = lax.optimization_barrier((asked, far))
    near = pack_near(listed, asked, query, key_rows)
    near = lax.all_to_all(near, "seq", split_axis=0, concat_axis=0, tiled=True)
    sent, place, most = send_near(near)
    sent, far, near = lax.optimization_barrier((sent, far, near))
    arrived_near = relay(sent)
    straight = [swap(far[m], 2 * m) for m in range(N_Y)]
    crossed = swap(jnp.stack([array[1] for array in straight]), 1)
    rows, cols = make_index(segment_ids.reshape(N_SEQ, ROWS), near)
    arrived_far = relay(send_far(ids, place, *straight, crossed))
    extra = lax.cond(
        most[0, 0] >= CAPACITY,
        lambda place, near, straight, crossed: relay(
            send_extra(ids, place, near, *straight, crossed)
        ),
        lambda place, near, straight, crossed: jnp.zeros((N_DP * EXTRA, 2 * HALF), jnp.bfloat16),
        place,
        near,
        straight,
        crossed,
    )
    held = weigh(segment_ids, most, arrived_near, extra, rows, cols)
    grads = back(segment_ids, most, arrived_far, extra, rows, cols, *held)
    returned = lax.all_to_all(
        grads.reshape(N_SEQ, ROWS, 4 * HEAD_DIM), "seq", split_axis=0, concat_axis=0, tiled=True
    )
    return unpack(returned)


def solution(mesh):
    in_specs = (
        P(("dp", "seq"), None),
        P(("dp", "seq"), None),
        P(("dp", "seq"), None),
        P(("dp", "seq"), None),
        P(("dp", "seq"), None),
        P(("dp", "seq")),
        P("dp"),
    )
    out_specs = (P(("dp", "seq"), None), P(("dp", "seq"), None), P(("dp", "seq"), None))
    return jax.shard_map(local, mesh=mesh, in_specs=in_specs, out_specs=out_specs, check_vma=False)
```

time: 271 us -> 178 us (0.66)
  local copies, waits for them, and re-layouts: 52.9 us -> 8.57 us
  waiting for transfers between devices: 107 us -> 63.7 us
  Pallas kernels: 0 us -> 33.7 us
  matrix products: 20.9 us -> 0 us
  other arithmetic: 10.4 us -> 0.07 us
  blocking collectives: 52.2 us -> 42.1 us
  starting transfers between devices: 23 us -> 27.7 us
    all_to_all x2 -> x3, waiting for transfers between devices: 107 us -> 53.8 us  [relay(): return lax.all_to_all(array, 'dp', split_axis=0, concat_axis=0, tiled=True)]
    all_gather x1 -> x0, blocking collectives: 33.8 us -> none  [local(): column_lists = lax.all_gather(source_row, 'dp', axis=0, tiled=True)]
    pallas_call x0 -> x9, Pallas kernels: none -> 33.7 us  [the longest x1 10.2 us: local(): grads = back(segment_ids, most, arrived_far, extra, rows, cols, *held)]
    scatter x2 -> x0, local copies, waits for them, and re-layouts: 31.2 us -> none  [the longest x1 15.7 us: local(): outgoing = jnp.zeros((dp_count * capacity,) + packed.shape[1:], packed.dt...]
    all_to_all x1 -> x2, blocking collectives: 18.3 us -> 42.1 us  [the longest x1 22.4 us: local(): lax.all_to_all(grads.reshape(N_SEQ, ROWS, 4 * HEAD_DIM), 'seq', split_axi...]
    dot_general x36 -> x0, matrix products: 20.9 us -> none  [the longest x6 7.28 us: tile_grads(): jnp.dot(grad_blk, value_blk.T, preferred_element_type=jnp.float32)]
    ppermute x0 -> x4, waiting for transfers between devices: none -> 9.9 us  [swap(): lax.ppermute(array, 'seq', [(s, s ^ m) for s in range(N_SEQ)])]
    ppermute x0 -> x4, starting transfers between devices: none -> 5.67 us  [swap(): lax.ppermute(array, 'seq', [(s, s ^ m) for s in range(N_SEQ)])]
  transfers between devices with their start and end apart: 2 -> 7, of which waited for: 2 -> 7; matrix products, arithmetic and copies ran while one was open for 1% -> 1% of each run, Pallas kernels for 0% -> 9%
where the time goes in v1:
time: 178 us; the launch traced here: 177 us
  waiting for transfers between devices  63.7 us (36%)
  blocking collectives  42.1 us (24%)
  Pallas kernels  33.7 us (19%)
  starting transfers between devices  27.7 us (16%)
  local copies, waits for them, and re-layouts  8.57 us (5%)
    all_to_all x3, waiting for transfers between devices, relay(): return lax.all_to_all(array, 'dp', split_axis=0, concat_axis=0, tiled=True)  53.8 us
    all_to_all x1, blocking collectives, local(): lax.all_to_all(grads.reshape(N_SEQ, ROWS, 4 * HEAD_DIM), 'seq', split_axi...  22.4 us
    all_to_all x3, starting transfers between devices, relay(): return lax.all_to_all(array, 'dp', split_axis=0, concat_axis=0, tiled=True)  22 us
    all_to_all x1, blocking collectives, local(): near = lax.all_to_all(near, 'seq', split_axis=0, concat_axis=0, tiled=True)  19.7 us
    pallas_call x1, Pallas kernels, local(): grads = back(segment_ids, most, arrived_far, extra, rows, cols, *held)  10.2 us
    ppermute x4, waiting for transfers between devices, swap(): lax.ppermute(array, 'seq', [(s, s ^ m) for s in range(N_SEQ)])  9.9 us
    unnamed x24, local copies, waits for them, and re-layouts  6.68 us
    pallas_call x1, Pallas kernels, local(): held = weigh(segment_ids, most, arrived_near, extra, rows, cols)  6.56 us
  transfers between devices with their start and end apart: 7, of which 7 were waited for; matrix products, arithmetic and copies ran while one was open for 1% of the time, Pallas kernels for 9%

profile of v1, /device:TPU:1, one launch (start us, length us, event | category | flops | bytes accessed | tf_op | source)
XLA Modules:
  0.0 177.3 jit_solution(18186944995877877662)
XLA Ops:
  0.6 0.0 copy-start.7
  0.6 0.6 copy-done.7
  1.3 1.1 request.1
  2.4 11.9 %all-to-all-start.1 = ((s32[32,1,128]{2,1,0:T(1,128)}), s32[32,1,128]{2,1,0:T(1,128)S(1)}, u32[]{:S(2)}, u32[]{:S(2)}) async-start(s32[32,1,128]{2,1,0:T(1,128)} %bitcast.4), calls=%async_computation.1 | async-start | bytes 32768 | tf_op jit(solution)/shard_map/all_to_all | solution.py:549
  14.2 2.5 %pack_far.1 = (bf16[2,136,384]{2,1,0:T(8,128)(2,1)S(1)}, bf16[2,136,384]{2,1,0:T(8,128)(2,1)}, bf16[2,136,384]{2,1,0:T(8,128)(2,1)}, bf16[2,136,384]{2,1,0:T(8,128)(2,1)}) custom-call(s32[1]{0:T(128)} %bitcast.6.ids_ref, bf16[128,1024]{1,0:T(8,128)(2,1)} %value_hbm.1, bf16[128,2048]{1,0:T(8,128)(2,1)} %out_hbm.1, bf16[128,2048]{1,0:T(8,128)(2,1)} %grad_hbm.1), custom_call_target="tpu_custom_call" | custom-call | tf_op jit(solution)/shard_map/pack_far/pallas_call | solution.py:560
  16.8 6.0 %all-to-all-done.1 = s32[32,1,128]{2,1,0:T(1,128)S(1)} async-done(((s32[32,1,128]{2,1,0:T(1,128)}), s32[32,1,128]{2,1,0:T(1,128)S(1)}, u32[]{:S(2)}, u32[]{:S(2)}) %all-to-all-start.1) | async-done | bytes 16416 | tf_op jit(solution)/shard_map/all_to_all | solution.py:549
  22.8 0.0 copy-start.8
  22.8 0.6 copy-done.8
  23.4 2.9 %pack_near.1 = bf16[8,136,384]{2,1,0:T(8,128)(2,1)} custom-call(s32[1,128]{1,0:T(1,128)} %bitcast.18, s32[32,128]{1,0:T(8,128)} %bitcast.22, bf16[128,2048]{1,0:T(8,128)(2,1)} %query_hbm.1, bf16[128,1024]{1,0:T(8,128)(2,1)} %key_hbm.1), custom_call_target="tpu_custom_call" | custom-call | tf_op jit(solution)/shard_map/pack_near/pallas_call | solution.py:562
  26.3 19.7 %all_to_all.54.rows_ref.head_ref = bf16[8,136,384]{2,1,0:T(8,128)(2,1)S(1)} all-to-all(bf16[8,136,384]{2,1,0:T(8,128)(2,1)} %pack_near.1), channel_id=1, replica_groups=mesh['dp'=32,'seq'=8] {'seq'}, dimensions={0} | all-to-all | bytes 1671168 | tf_op jit(solution)/shard_map/all_to_all | solution.py:563
  46.0 0.0 copy-start.11
  46.0 0.0 copy-start.10
  46.0 0.0 copy-start.9
  46.0 3.3 %send_near.1 = (bf16[1792,384]{1,0:T(8,128)(2,1)}, f32[8,1024]{1,0:T(8,128)S(1)}, s32[1,1]{1,0:T(1,128)}) custom-call(bf16[8,136,384]{2,1,0:T(8,128)(2,1)S(1)} %all_to_all.54.rows_ref.head_ref), custom_call_target="tpu_custom_call" | custom-call | flops 1400000000 | bytes 4000000 | tf_op jit(solution)/shard_map/send_near/pallas_call | solution.py:564
  49.3 0.0 copy-done.11
  49.3 0.4 collective-permute-start
  49.7 0.0 copy-done.10
  49.7 1.8 %collective-permute-start.1 = (bf16[2,136,384]{2,1,0:T(8,128)(2,1)S(1)}, bf16[2,136,384]{2,1,0:T(8,128)(2,1)}, u32[]{:S(2)}, u32[]{:S(2)}) collective-permute-start(bf16[2,136,384]{2,1,0:T(8,128)(2,1)S(1)} %copy-done.10), channel_id=1, source_target_pairs={{0,4},{1,5},{2,6},{3,7},{4,0},{5,1},{6,2},{7,3},{8,12},{9,13},{10,... | collective-permute-start | bytes 626696 | tf_op jit(solution)/shard_map/ppermute | solution.py:553
  51.5 0.0 copy-done.9
  51.5 1.8 %collective-permute-start.2 = (bf16[2,136,384]{2,1,0:T(8,128)(2,1)S(1)}, bf16[2,136,384]{2,1,0:T(8,128)(2,1)}, u32[]{:S(2)}, u32[]{:S(2)}) collective-permute-start(bf16[2,136,384]{2,1,0:T(8,128)(2,1)S(1)} %copy-done.9), channel_id=1, source_target_pairs={{0,6},{1,7},{2,4},{3,5},{4,2},{5,3},{6,0},{7,1},{8,14},{9,15},{10,... | collective-permute-start | bytes 626696 | tf_op jit(solution)/shard_map/ppermute | solution.py:553
  53.3 2.2 %collective-permute-done.refs_1_ = bf16[2,136,384]{2,1,0:T(8,128)(2,1)S(1)} collective-permute-done((bf16[2,136,384]{2,1,0:T(8,128)(2,1)S(1)}, bf16[2,136,384]{2,1,0:T(8,128)(2,1)S(1)}, u32[]{:S(2)}, u32[]{:S(2)}) %collective-permute-start) | collective-permute-done | bytes 208928 | tf_op jit(solution)/shard_map/ppermute | solution.py:553
  55.5 5.2 %collective-permute-done.1.refs_2_ = bf16[2,136,384]{2,1,0:T(8,128)(2,1)} collective-permute-done((bf16[2,136,384]{2,1,0:T(8,128)(2,1)S(1)}, bf16[2,136,384]{2,1,0:T(8,128)(2,1)}, u32[]{:S(2)}, u32[]{:S(2)}) %collective-permute-start.1) | collective-permute-done | bytes 208928 | tf_op jit(solution)/shard_map/ppermute | solution.py:553
  60.7 0.9 slice.17
  61.6 1.6 collective-permute-done.2.refs_3_
  63.2 0.9 slice.18
  64.1 0.1 pad_maximum_fusion
  64.2 1.7 collective-permute-start.3
  66.6 0.9 collective-permute-done.3.refs_4_
  67.4 0.1 conditional.1
  67.4 0.1 broadcast.2
  67.5 4.0 %all-to-all-start.4 = ((bf16[32,56,384]{2,1,0:T(8,128)(2,1)}), bf16[32,56,384]{2,1,0:T(8,128)(2,1)S(1)}, u32[]{:S(2)}, u32[]{:S(2)}) async-start(bf16[32,56,384]{2,1,0:T(8,128)(2,1)} %bitcast.11), calls=%async_computation.4 | async-start | bytes 2752512 | tf_op jit(solution)/shard_map/all_to_all | solution.py:549
  71.5 5.0 %send_far.1 = bf16[1792,384]{1,0:T(8,128)(2,1)} custom-call(s32[1]{0:T(128)} %bitcast.6.ids_ref, f32[8,1024]{1,0:T(8,128)S(1)} %get-tuple-element.60.place_ref, bf16[2,136,384]{2,1,0:T(8,128)(2,1)S(1)} %get-tuple-element.66.refs_0_, bf16[2,136,384]{2,1,0:T(8,128)(2,1)S(1)} %collective-permute-done.refs_1_, ...), custom_call_target="tpu_custom_call" | custom-call | flops 1400000000 | bytes 4000000 | tf_op jit(solution)/shard_map/send_far/pallas_call | solution.py:570
  76.5 29.1 %all-to-all-done.4 = bf16[32,56,384]{2,1,0:T(8,128)(2,1)S(1)} async-done(((bf16[32,56,384]{2,1,0:T(8,128)(2,1)}), bf16[32,56,384]{2,1,0:T(8,128)(2,1)S(1)}, u32[]{:S(2)}, u32[]{:S(2)}) %all-to-all-start.4) | async-done | bytes 1376288 | tf_op jit(solution)/shard_map/all_to_all | solution.py:549
  105.6 0.0 copy-start.5
  105.6 6.2 %all-to-all-start.3 = ((bf16[32,56,384]{2,1,0:T(8,128)(2,1)}), bf16[32,56,384]{2,1,0:T(8,128)(2,1)}, u32[]{:S(2)}, u32[]{:S(2)}) async-start(bf16[32,56,384]{2,1,0:T(8,128)(2,1)} %bitcast.7), calls=%async_computation.3 | async-start | bytes 2752512 | tf_op jit(solution)/shard_map/all_to_all | solution.py:549
  111.8 0.0 copy-done.5
  111.8 1.0 index.1
  112.8 0.0 copy-start.3
  112.8 0.0 copy-start.6
  112.8 6.6 %weigh.1 = (bf16[1024,384]{1,0:T(8,128)(2,1)S(1)}, bf16[128,1024]{1,0:T(8,128)(2,1)S(1)}, bf16[2560,512]{1,0:T(8,128)(2,1)S(1)}, f32[2560,512]{1,0:T(8,128)S(1)}) custom-call(s32[1024]{0:T(1024)S(1)} %copy-done.5, s32[1,1]{1,0:T(1,128)} %get-tuple-element.59.most_ref, bf16[1792,384]{1,0:T(8,128)(2,1)S(1)} %bitcast.16, ...), custom_call_target="tpu_custom_call" | custom-call | flops 3000000000 | bytes 4000000 | tf_op jit(solution)/shard_map/weigh/pallas_call | solution.py:582
  119.4 0.0 copy-done.3
  119.4 0.0 copy-done.6
  119.4 0.0 copy-start
  119.4 2.3 %copy-done = f32[2560,512]{1,0:T(8,128)} copy-done((f32[2560,512]{1,0:T(8,128)}, f32[2560,512]{1,0:T(8,128)S(1)}, u32[]{:S(2)}) %copy-start) | copy-done | bytes 5242904
  121.8 0.0 copy-start.1
  121.8 1.5 copy-done.1
  123.3 0.0 copy-start.2
  123.3 0.9 copy-done.2
  124.1 0.0 copy-start.4
  124.1 0.7 copy-done.4
  124.8 18.7 %all-to-all-done.3 = bf16[32,56,384]{2,1,0:T(8,128)(2,1)} async-done(((bf16[32,56,384]{2,1,0:T(8,128)(2,1)}), bf16[32,56,384]{2,1,0:T(8,128)(2,1)}, u32[]{:S(2)}, u32[]{:S(2)}) %all-to-all-start.3) | async-done | bytes 1376288 | tf_op jit(solution)/shard_map/all_to_all | solution.py:549
  143.5 10.2 %back.1 = bf16[1024,512]{1,0:T(8,128)(2,1)} custom-call(s32[1024]{0:T(1024)} %segment_ref.3, s32[1,1]{1,0:T(1,128)} %get-tuple-element.59.most_ref, bf16[1792,384]{1,0:T(8,128)(2,1)} %bitcast.8.arrived_ref, bf16[512,768]{1,0:T(8,128)(2,1)S(1)} %get-tuple-element.78.extra_hbm, f32[24,128]{1,0:T(8,128)} %copy-done.6, f32[1024,128]{1,0:T(8,128)} %copy-done.3, ...), custom_call_target="tpu_custom_call" | custom-call | tf_op jit(solution)/shard_map/back/pallas_call | solution.py:583
  153.7 22.4 %all_to_all.55.returned_ref = bf16[8,128,512]{2,1,0:T(8,128)(2,1)S(1)} all-to-all(bf16[8,128,512]{2,1,0:T(8,128)(2,1)} %bitcast.20), channel_id=1, replica_groups=mesh['dp'=32,'seq'=8] {'seq'}, dimensions={0} | all-to-all | bytes 2097152 | tf_op jit(solution)/shard_map/all_to_all | solution.py:584
  176.2 1.2 unpack.1
  (2 shorter events, 0.0 us)
Async XLA Ops:
  0.6 0.7 copy-start.7
  2.4 20.4 %all-to-all-start.1 = ((s32[32,1,128]{2,1,0:T(1,128)}), s32[32,1,128]{2,1,0:T(1,128)S(1)}, u32[]{:S(2)}, u32[]{:S(2)}) async-start(s32[32,1,128]{2,1,0:T(1,128)} %bitcast.4), calls=%async_computation.1 | async-start | bytes 32768 | tf_op jit(solution)/shard_map/all_to_all | solution.py:549
  22.8 0.6 copy-start.8
  46.0 3.3 %copy-start.11 = (bf16[2,136,384]{2,1,0:T(8,128)(2,1)S(1)}, bf16[2,136,384]{2,1,0:T(8,128)(2,1)}, u32[]{:S(2)}) copy-start(bf16[2,136,384]{2,1,0:T(8,128)(2,1)} %get-tuple-element.67) | copy-start | bytes 626692
  46.0 3.7 %copy-start.10 = (bf16[2,136,384]{2,1,0:T(8,128)(2,1)S(1)}, bf16[2,136,384]{2,1,0:T(8,128)(2,1)}, u32[]{:S(2)}) copy-start(bf16[2,136,384]{2,1,0:T(8,128)(2,1)} %get-tuple-element.68) | copy-start | bytes 626692
  46.0 5.5 %copy-start.9 = (bf16[2,136,384]{2,1,0:T(8,128)(2,1)S(1)}, bf16[2,136,384]{2,1,0:T(8,128)(2,1)}, u32[]{:S(2)}) copy-start(bf16[2,136,384]{2,1,0:T(8,128)(2,1)} %get-tuple-element.69) | copy-start | bytes 626692
  49.3 6.1 %collective-permute-start = (bf16[2,136,384]{2,1,0:T(8,128)(2,1)S(1)}, bf16[2,136,384]{2,1,0:T(8,128)(2,1)S(1)}, u32[]{:S(2)}, u32[]{:S(2)}) collective-permute-start(bf16[2,136,384]{2,1,0:T(8,128)(2,1)S(1)} %copy-done.11), channel_id=1, source_target_pairs={{0,2},{1,3},{2,0},{3,1},{4,6},{5,7},{6,4},{7,5},{8,10},{9,11},{10,... | collective-permute-start | bytes 626696 | tf_op jit(solution)/shard_map/ppermute | solution.py:553
  49.7 11.0 %collective-permute-start.1 = (bf16[2,136,384]{2,1,0:T(8,128)(2,1)S(1)}, bf16[2,136,384]{2,1,0:T(8,128)(2,1)}, u32[]{:S(2)}, u32[]{:S(2)}) collective-permute-start(bf16[2,136,384]{2,1,0:T(8,128)(2,1)S(1)} %copy-done.10), channel_id=1, source_target_pairs={{0,4},{1,5},{2,6},{3,7},{4,0},{5,1},{6,2},{7,3},{8,12},{9,13},{10,... | collective-permute-start | bytes 626696 | tf_op jit(solution)/shard_map/ppermute | solution.py:553
  51.5 11.7 %collective-permute-start.2 = (bf16[2,136,384]{2,1,0:T(8,128)(2,1)S(1)}, bf16[2,136,384]{2,1,0:T(8,128)(2,1)}, u32[]{:S(2)}, u32[]{:S(2)}) collective-permute-start(bf16[2,136,384]{2,1,0:T(8,128)(2,1)S(1)} %copy-done.9), channel_id=1, source_target_pairs={{0,6},{1,7},{2,4},{3,5},{4,2},{5,3},{6,0},{7,1},{8,14},{9,15},{10,... | collective-permute-start | bytes 626696 | tf_op jit(solution)/shard_map/ppermute | solution.py:553
  64.2 3.2 %collective-permute-start.3 = (bf16[4,136,384]{2,1,0:T(8,128)(2,1)S(1)}, bf16[4,136,384]{2,1,0:T(8,128)(2,1)}, u32[]{:S(2)}, u32[]{:S(2)}) collective-permute-start(bf16[4,136,384]{2,1,0:T(8,128)(2,1)S(1)} %pad_maximum_fusion), channel_id=1, source_target_pairs={{0,1},{1,0},{2,3},{3,2},{4,5},{5,4},{6,7},{7,6},{8,9},{9,8},{10,11... | collective-permute-start | bytes 1253384 | tf_op jit(solution)/shard_map/ppermute | solution.py:553
  67.5 38.1 %all-to-all-start.4 = ((bf16[32,56,384]{2,1,0:T(8,128)(2,1)}), bf16[32,56,384]{2,1,0:T(8,128)(2,1)S(1)}, u32[]{:S(2)}, u32[]{:S(2)}) async-start(bf16[32,56,384]{2,1,0:T(8,128)(2,1)} %bitcast.11), calls=%async_computation.4 | async-start | bytes 2752512 | tf_op jit(solution)/shard_map/all_to_all | solution.py:549
  105.6 6.2 %copy-start.5 = (s32[1024]{0:T(1024)S(1)}, s32[1024]{0:T(1024)}, u32[]{:S(2)}) copy-start(s32[1024]{0:T(1024)} %segment_ref.3) | copy-start | bytes 12292
  105.6 37.9 %all-to-all-start.3 = ((bf16[32,56,384]{2,1,0:T(8,128)(2,1)}), bf16[32,56,384]{2,1,0:T(8,128)(2,1)}, u32[]{:S(2)}, u32[]{:S(2)}) async-start(bf16[32,56,384]{2,1,0:T(8,128)(2,1)} %bitcast.7), calls=%async_computation.3 | async-start | bytes 2752512 | tf_op jit(solution)/shard_map/all_to_all | solution.py:549
  112.8 6.6 %copy-start.3 = (f32[1024,128]{1,0:T(8,128)}, f32[1024,128]{1,0:T(8,128)S(1)}, u32[]{:S(2)}) copy-start(f32[1024,128]{1,0:T(8,128)S(1)} %get-tuple-element.72.cols_ref) | copy-start | bytes 1572868
  112.8 6.6 %copy-start.6 = (f32[24,128]{1,0:T(8,128)}, f32[24,128]{1,0:T(8,128)S(1)}, u32[]{:S(2)}) copy-start(f32[24,128]{1,0:T(8,128)S(1)} %get-tuple-element.71.rows_ref) | copy-start | bytes 36868
  119.4 2.3 %copy-start = (f32[2560,512]{1,0:T(8,128)}, f32[2560,512]{1,0:T(8,128)S(1)}, u32[]{:S(2)}) copy-start(f32[2560,512]{1,0:T(8,128)S(1)} %get-tuple-element.77.slope_hbm) | copy-start | bytes 15728644
  121.8 1.5 copy-start.1
  123.3 0.9 copy-start.2
  124.1 0.7 copy-start.4
